TPU v7x, 32 devices: a whole 2x2x4 slice. The times are simulated.
32 devices in a mesh: slab: 4 (over y, x), angle: 8 (over z, core).
Axes of the slice: x: 2, y: 2, z: 4, core: 2. Of those that a mesh axis runs over, the one named last changes fastest.
Arguments:
- volume: bfloat16 [32, 32, 2048], P('slab', 'angle'), may hold values from -6 to 6
- measured: float32 [8, 32, 2048], P('angle', 'slab'), may hold values from -6 to 6
- ray_tiles: bfloat16 [8, 32, 2, 128, 128], P(None, 'angle'), may hold values from -0.0625 to 0.0625
- tile_offsets: int32 [8, 32], replicated, may hold values from -3 to 3
- band_counts: int32 [8, 32], replicated, may hold values from 1 to 2
Outputs:
- updated: float32 [32, 32, 2048], P('slab', 'angle')
- residual: float32 [8, 32, 2048], P('angle', 'slab')
All inputs are finite; a program needn't handle non-finite values.
Results may differ from a plain program's by a relative error of at most 0.00056.
Values may be sent and summed in bfloat16 or wider, within the bound.
A program may use at most 64 MiB of HBM per device.

v0:
```python
from functools import partial

import jax
import jax.numpy as jnp
from jax import lax
from jax.sharding import PartitionSpec as P

OFFMAX = 3


step_size = 0.3
smooth_weight = 0.2
smooth_floor = 0.25


def padded_2(shard, sides, width):
    for axis, dim in sides:
        size, length = (lax.axis_size(axis), shard.shape[dim])
        up = [(i, (i + 1) % size) for i in range(size - 1)]
        down = [(j, i) for i, j in up]
        last = lax.slice_in_dim(shard, length - width, length, axis=dim)
        initial = lax.slice_in_dim(shard, 0, width, axis=dim)
        before = lax.ppermute(last, axis, up)
        after = lax.ppermute(initial, axis, down)
        shard = jnp.concatenate([before, shard, after], axis=dim)
    return shard


def shift_table(tile_offsets, band_counts, band):
    center = band // 2
    shifts = jnp.stack([tile_offsets + (k - center) for k in range(band)], axis=1)
    masks = jnp.stack([band_counts > k for k in range(band)], axis=1).astype(jnp.bfloat16)
    return (shifts, masks)


def project_angle(padded, shifts, masks, tiles, margin):
    tile_count = padded.shape[2] - 2 * margin
    summed = jnp.zeros((padded.shape[0], tile_count, padded.shape[3]), jnp.float32)
    for k in range(tiles.shape[1]):
        moved = jax.vmap(
            lambda block, offset: lax.dynamic_slice_in_dim(block, margin + offset, tile_count, 1),
            in_axes=(1, 0),
            out_axes=1,
        )(padded, shifts[k])
        moved = moved * masks[k][None, :, None, None]
        summed = summed + jnp.einsum(
            "zrtc,rcd->ztd", moved, tiles[:, k], preferred_element_type=jnp.float32
        )
    return summed.reshape(padded.shape[0], tile_count * padded.shape[3])


def spread_angle(view_pad, shifts, masks, tiles, margin):
    tile_count = view_pad.shape[1] - 2 * margin
    rows_here = shifts.shape[1]
    summed = jnp.zeros((view_pad.shape[0], rows_here, tile_count, view_pad.shape[2]), jnp.float32)
    for k in range(tiles.shape[1]):
        moved = jax.vmap(
            lambda offset: lax.dynamic_slice_in_dim(view_pad, margin - offset, tile_count, 1),
            out_axes=1,
        )(shifts[k])
        product = jnp.einsum(
            "zrtd,rcd->zrtc", moved, tiles[:, k], preferred_element_type=jnp.float32
        )
        summed = summed + product * masks[k].astype(jnp.float32)[None, :, None, None]
    return summed.reshape(view_pad.shape[0], rows_here, tile_count * view_pad.shape[2])


def divergence(field):
    base = field[:-1, :-1, :-1]
    step_z = field[1:, :-1, :-1] - base
    step_y = field[:-1, 1:, :-1] - base
    step_x = field[:-1, :-1, 1:] - base
    scale = jnp.sqrt(step_z * step_z + step_y * step_y + step_x * step_x + smooth_floor)
    flow_z = step_z / scale
    flow_y = step_y / scale
    flow_x = step_x / scale
    result = flow_z[1:, 1:, 1:] - flow_z[:-1, 1:, 1:]
    result = result + flow_y[1:, 1:, 1:] - flow_y[1:, :-1, 1:]
    return result + flow_x[1:, 1:, 1:] - flow_x[1:, 1:, :-1]


def per_device(volume, measured, ray_tiles, tile_offsets, band_counts):
    depth, row_count, width = volume.shape
    band = ray_tiles.shape[2]
    tile = ray_tiles.shape[3]
    margin = OFFMAX + band
    tile_count = width // tile
    angle_dev = measured.shape[0]
    first_angle = lax.axis_index("angle") * angle_dev
    first_row = lax.axis_index("angle") * row_count
    shifts, masks = shift_table(tile_offsets, band_counts, band)
    row_shifts = lax.dynamic_slice_in_dim(shifts, first_row, row_count, 2)
    row_masks = lax.dynamic_slice_in_dim(masks, first_row, row_count, 2)
    blocks = volume.reshape(depth, row_count, tile_count, tile)
    padded = jnp.pad(blocks, ((0, 0), (0, 0), (margin, margin), (0, 0)))
    sub_shift = row_shifts
    sub_mask = row_masks
    sub_tiles = ray_tiles
    full_views = lax.psum(
        jax.vmap(partial(project_angle, margin=margin), in_axes=(None, 0, 0, 0))(
            padded, sub_shift, sub_mask, sub_tiles
        ),
        "angle",
    )
    measured_all = lax.all_gather(measured, "angle", axis=0, tiled=True)
    residual_all = full_views - measured_all
    residual = lax.dynamic_slice_in_dim(residual_all, first_angle, angle_dev, 0)
    rounded_all = residual_all.astype(jnp.bfloat16)
    count = rounded_all.shape[0]
    sub_shift = row_shifts
    sub_mask = row_masks
    sub_tiles = ray_tiles
    view_blocks = rounded_all.reshape(count, rounded_all.shape[1], tile_count, tile)
    view_pad = jnp.pad(view_blocks, ((0, 0), (0, 0), (margin, margin), (0, 0)))
    spread = jax.vmap(partial(spread_angle, margin=margin))(
        view_pad, sub_shift, sub_mask, sub_tiles
    )
    gradient = jnp.sum(spread, axis=0)
    beside_all = padded_2(volume, (("slab", 0), ("angle", 1)), 1)
    field = jnp.pad(beside_all.astype(jnp.float32), ((0, 0), (0, 0), (1, 1)))
    updated = (
        volume.astype(jnp.float32)
        - step_size * gradient
        + step_size * smooth_weight * divergence(field)
    )
    return (updated, residual)


def solution(mesh):
    return jax.shard_map(
        per_device,
        mesh=mesh,
        in_specs=(
            P("slab", "angle", None),
            P("angle", "slab", None),
            P(None, "angle", None, None, None),
            P(),
            P(),
        ),
        out_specs=(P("slab", "angle", None), P("angle", "slab", None)),
        check_vma=False,
    )
```

profile of v0, /device:TPU:0, one launch (start us, length us, event | category | flops | bytes accessed | tf_op | source)
XLA Modules:
  0.0 96.6 jit_solution(14420413369524274405)
XLA Ops:
  7.2 0.7 add_bitcast_fusion
  7.9 0.8 dynamic-slice_add_fusion
  9.2 1.0 %reshape.176 = bf16[8,4,16,128]{3,2,1,0:T(8,128)(2,1)S(1)} reshape(bf16[8,4,2048]{2,1,0:T(4,128)(2,1)} %param.5) | data formatting | bytes 262144 | tf_op jit(solution)/shard_map/reshape | solution.py:94
  10.2 0.1 copy.59
  10.3 0.7 compare_bitcast_fusion.1
  11.1 0.1 copy.70
  11.2 0.1 copy.71
  11.4 0.9 gather_fusion.1
  12.4 0.9 gather_fusion
  13.3 0.1 copy.63
  13.4 0.1 copy.64
  13.5 1.9 %convolution_bitcast_fusion = f32[8,8,16,128]{3,2,1,0:T(8,128)S(1)} fusion(bf16[8,4,8,16,128]{4,2,3,1,0:T(8,128)(2,1)S(1)} %bitcast.101, bf16[8,4,2,128,128]{4,3,2,1,0:T(8,128)(2,1)} %param.7, bf16[8,4]{1,0:T(8,128)(2,1)S(1)} %copy.71), kind=kOutput, calls=%fused_computation.5 | convolution fusion | flops 134742016 | bytes 2621504 | tf_op jit(solution)/shard_map/vmap(zrtc,rcd->ztd)/dot_general | solution.py:46
  15.4 0.5 fusion
  15.9 0.9 reshape.146
  16.8 4.8 %collective-permute-start = (bf16[1,4,2048]{2,1,0:T(4,128)(2,1)S(1)}, bf16[1,4,2048]{2,1,0:T(4,128)(2,1)S(1)}, u32[]{:S(2)}, u32[]{:S(2)}) collective-permute-start(bf16[1,4,2048]{2,1,0:T(4,128)(2,1)S(1)} %get-tuple-element.11), channel_id=1, source_target_pairs={{0,8},{8,16},{16,24},{1,9},{9,17},{17,25},{2,10},{10,18},{18,26},{... | collective-permute-start | bytes 49160 | tf_op jit(solution)/shard_map/ppermute | solution.py:23
  21.7 1.3 %collective-permute-start.1 = (bf16[1,4,2048]{2,1,0:T(4,128)(2,1)S(1)}, bf16[1,4,2048]{2,1,0:T(4,128)(2,1)S(1)}, u32[]{:S(2)}, u32[]{:S(2)}) collective-permute-start(bf16[1,4,2048]{2,1,0:T(4,128)(2,1)S(1)} %get-tuple-element.10), channel_id=1, source_target_pairs={{8,0},{16,8},{24,16},{9,1},{17,9},{25,17},{10,2},{18,10},{26,18},{... | collective-permute-start | bytes 49160 | tf_op jit(solution)/shard_map/ppermute | solution.py:24
  23.0 15.9 %all_gather.3 = f32[8,8,2048]{2,1,0:T(8,128)S(1)} all-gather(f32[1,8,2048]{2,1,0:T(8,128)S(1)} %copy-done.3), channel_id=1, replica_groups=mesh['slab'=4,'angle'=8] {'angle'}, dimensions={0}, use_global_device_ids=true | all-gather | bytes 589824 | tf_op jit(solution)/shard_map/all_gather | solution.py:105
  39.3 0.1 fusion.43
  39.5 2.3 %collective-permute-start.2 = (bf16[10,1,2048]{2,1,0:T(2,128)(2,1)S(1)}, bf16[10,1,2048]{2,1,0:T(2,128)(2,1)S(1)}, u32[]{:S(2)}, u32[]{:S(2)}) collective-permute-start(bf16[10,1,2048]{2,1,0:T(2,128)(2,1)S(1)} %get-tuple-element.8), channel_id=1, source_target_pairs={{0,1},{1,2},{2,3},{3,4},{4,5},{5,6},{6,7},{8,9},{9,10},{10,11},{11... | collective-permute-start | bytes 122888 | tf_op jit(solution)/shard_map/ppermute | solution.py:23
  41.7 1.3 %collective-permute-start.3 = (bf16[10,1,2048]{2,1,0:T(2,128)(2,1)S(1)}, bf16[10,1,2048]{2,1,0:T(2,128)(2,1)S(1)}, u32[]{:S(2)}, u32[]{:S(2)}) collective-permute-start(bf16[10,1,2048]{2,1,0:T(2,128)(2,1)S(1)} %get-tuple-element.9), channel_id=1, source_target_pairs={{1,0},{2,1},{3,2},{4,3},{5,4},{6,5},{7,6},{9,8},{10,9},{11,10},{12... | collective-permute-start | bytes 122888 | tf_op jit(solution)/shard_map/ppermute | solution.py:24
  43.5 2.2 %collective-permute-done.3 = bf16[10,1,2048]{2,1,0:T(2,128)(2,1)S(1)} collective-permute-done((bf16[10,1,2048]{2,1,0:T(2,128)(2,1)S(1)}, bf16[10,1,2048]{2,1,0:T(2,128)(2,1)S(1)}, u32[]{:S(2)}, u32[]{:S(2)}) %collective-permute-start.3) | collective-permute-done | bytes 40992 | tf_op jit(solution)/shard_map/ppermute | solution.py:24
  45.8 0.5 fusion.24
  46.3 0.5 fusion.27
  46.8 0.3 fusion.28
  47.0 29.5 %all-reduce.5.cloned.1.call-done = f32[8,8,2048]{2,1,0:T(8,128)} async-done(((f32[8,8,2048]{2,1,0:T(8,128)}), f32[8,8,2048]{2,1,0:T(8,128)}) %all-reduce.5.cloned.1.call-update) | async-done | bytes 524304 | tf_op jit(solution)/shard_map/psum | solution.py:99
  76.5 1.9 %convert_bitcast_fusion = (bf16[8,1,16,8,128]{4,3,2,1,0:T(8,128)(2,1)S(1)}, f32[8,8,2048]{2,1,0:T(8,128)}) fusion(f32[8,8,2048]{2,1,0:T(8,128)} %all-reduce.5.cloned.1.call-done, f32[8,8,2048]{2,1,0:T(8,128)S(1)} %all_gather.3), kind=kLoop, calls=%fused_computation.50 | loop fusion | flops 262144 | bytes 1835008
  78.6 0.9 gather_fusion.2
  79.5 3.4 %fusion.2 = f32[8,4,8,16,128]{4,3,2,1,0:T(8,128)} fusion(bf16[8,4,8,16,128]{4,2,3,1,0:T(8,128)(2,1)S(1)} %bitcast.100, bf16[8,4,2,128,128]{4,3,2,1,0:T(8,128)(2,1)} %param.7), kind=kOutput, calls=%fused_computation.9 | convolution fusion | flops 134217728 | bytes 4194304 | tf_op jit(solution)/shard_map/vmap(zrtd,rcd->zrtc)/dot_general | solution.py:61
  82.9 0.9 gather_fusion.3
  83.9 2.8 %add_reduce_fusion = f32[4,8,16,128]{3,2,1,0:T(8,128)S(1)} fusion(f32[8,4,8,16,128]{4,3,2,1,0:T(8,128)} %fusion.2, bf16[8,4,8,16,128]{4,2,3,1,0:T(8,128)(2,1)S(1)} %bitcast.103, f32[8,4]{1,0:T(8,128)S(1)} %copy.84, f32[8,4]{1,0:T(8,128)S(1)} %copy.79, bf16[8,4,2,128,128]{4,3,2,1,0:T(8,128)(2,1)} %param.7), kind=kOutput, calls=%fused_computation.4 | convolution fusion | flops 136249344 | bytes 4456704 | tf_op jit(solution)/shard_map/vmap(zrtd,rcd->zrtc)/dot_general | solution.py:61
  86.8 1.5 %constant_dynamic-slice_fusion = f32[1,8,2048]{2,1,0:T(8,128)} fusion(f32[8,8,2048]{2,1,0:T(8,128)} %get-tuple-element.3, s32[]{:T(128)S(6)} %select_n.52), kind=kLoop, calls=%fused_computation.90 | loop fusion | bytes 131076 | tf_op jit(solution)/shard_map/dynamic_slice | solution.py:107
  88.3 1.5 %fusion.26 = f32[8,4,2048]{2,1,0:T(4,128)} fusion(f32[9,5,2049]{2,1,0:T(8,128)S(1)} %get-tuple-element.7, f32[9,5,2049]{2,1,0:T(8,128)S(1)} %get-tuple-element.6, f32[9,5,2049]{2,1,0:T(8,128)S(1)} %get-tuple-element.4, f32[8,4,2048]{2,0,1:T(8,128)S(1)} %mul.90, bf16[8,4,2048]{2,1,0:T(4,128)(2,1)S(1)} %copy-done.1), kind=kLoop, calls=%fused_computation.43 | loop fusion | flops 589824 | bytes 2228224 | tf_op jit(solution)/shard_map/add | solution.py:122
  (47 shorter events, 2.0 us)
Async XLA Ops:
  7.2 69.4 %all-reduce.5.cloned.1.call-start = ((), (), s32[]{:S(2)}) async-start(), calls=%async_computation | async-start | bytes 1048576 | tf_op jit(solution)/shard_map/psum | solution.py:99
  13.5 1.9 %copy-start.2 = (bf16[8,4,2,128,128]{4,3,2,1,0:T(8,128)(2,1)S(1)}, bf16[8,4,2,128,128]{4,3,2,1,0:T(8,128)(2,1)}, u32[]{:S(2)}) copy-start(bf16[8,4,2,128,128]{4,3,2,1,0:T(8,128)(2,1)} %param.7) | copy-start | bytes 6291460
  15.4 1.4 %copy-start = (bf16[8,4,2048]{2,1,0:T(4,128)(2,1)S(1)}, bf16[8,4,2048]{2,1,0:T(4,128)(2,1)}, u32[]{:S(2)}) copy-start(bf16[8,4,2048]{2,1,0:T(4,128)(2,1)} %param.5) | copy-start | bytes 393220
  15.4 7.6 %copy-start.3 = (f32[1,8,2048]{2,1,0:T(8,128)S(1)}, f32[1,8,2048]{2,1,0:T(8,128)}, u32[]{:S(2)}) copy-start(f32[1,8,2048]{2,1,0:T(8,128)} %param.6) | copy-start | bytes 196612
  16.8 22.4 %collective-permute-start = (bf16[1,4,2048]{2,1,0:T(4,128)(2,1)S(1)}, bf16[1,4,2048]{2,1,0:T(4,128)(2,1)S(1)}, u32[]{:S(2)}, u32[]{:S(2)}) collective-permute-start(bf16[1,4,2048]{2,1,0:T(4,128)(2,1)S(1)} %get-tuple-element.11), channel_id=1, source_target_pairs={{0,8},{8,16},{16,24},{1,9},{9,17},{17,25},{2,10},{10,18},{18,26},{... | collective-permute-start | bytes 49160 | tf_op jit(solution)/shard_map/ppermute | solution.py:23
  21.7 17.7 %collective-permute-start.1 = (bf16[1,4,2048]{2,1,0:T(4,128)(2,1)S(1)}, bf16[1,4,2048]{2,1,0:T(4,128)(2,1)S(1)}, u32[]{:S(2)}, u32[]{:S(2)}) collective-permute-start(bf16[1,4,2048]{2,1,0:T(4,128)(2,1)S(1)} %get-tuple-element.10), channel_id=1, source_target_pairs={{8,0},{16,8},{24,16},{9,1},{17,9},{25,17},{10,2},{18,10},{26,18},{... | collective-permute-start | bytes 49160 | tf_op jit(solution)/shard_map/ppermute | solution.py:24
  39.5 4.1 %collective-permute-start.2 = (bf16[10,1,2048]{2,1,0:T(2,128)(2,1)S(1)}, bf16[10,1,2048]{2,1,0:T(2,128)(2,1)S(1)}, u32[]{:S(2)}, u32[]{:S(2)}) collective-permute-start(bf16[10,1,2048]{2,1,0:T(2,128)(2,1)S(1)} %get-tuple-element.8), channel_id=1, source_target_pairs={{0,1},{1,2},{2,3},{3,4},{4,5},{5,6},{6,7},{8,9},{9,10},{10,11},{11... | collective-permute-start | bytes 122888 | tf_op jit(solution)/shard_map/ppermute | solution.py:23
  41.7 4.0 %collective-permute-start.3 = (bf16[10,1,2048]{2,1,0:T(2,128)(2,1)S(1)}, bf16[10,1,2048]{2,1,0:T(2,128)(2,1)S(1)}, u32[]{:S(2)}, u32[]{:S(2)}) collective-permute-start(bf16[10,1,2048]{2,1,0:T(2,128)(2,1)S(1)} %get-tuple-element.9), channel_id=1, source_target_pairs={{1,0},{2,1},{3,2},{4,3},{5,4},{6,5},{7,6},{9,8},{10,9},{11,10},{12... | collective-permute-start | bytes 122888 | tf_op jit(solution)/shard_map/ppermute | solution.py:24
  83.9 4.4 %copy-start.1 = (bf16[8,4,2048]{2,1,0:T(4,128)(2,1)S(1)}, bf16[8,4,2048]{2,1,0:T(4,128)(2,1)}, u32[]{:S(2)}) copy-start(bf16[8,4,2048]{2,1,0:T(4,128)(2,1)} %param.5) | copy-start | bytes 393220
Sparse Core Ops, SparseCore 0:
  16.9 59.5 all-reduce.4
where the time goes:
time: 97.1 us; the launch traced here: 96.6 us
  waiting for transfers between devices  31.7 us (33%)
  blocking collectives  15.9 us (16%)
  between operations  14.3 us (15%)
  starting transfers between devices  9.72 us (10%)
  local copies, waits for them, and re-layouts  9.46 us (10%)
  matrix products  8.57 us (9%)
  other arithmetic  6.94 us (7%)
    psum x1, waiting for transfers between devices, per_device(): lax.psum(jax.vmap(partial(project_angle, margin=margin), in_axes=(None, 0...  29.5 us
    all_gather x1, blocking collectives, per_device(): measured_all = lax.all_gather(measured, 'angle', axis=0, tiled=True)  15.9 us
    ppermute x2, starting transfers between devices, padded_2(): before = lax.ppermute(last, axis, up)  7.09 us
    dot_general x2, matrix products, spread_angle(): jnp.einsum('zrtd,rcd->zrtc', moved, tiles[:, k], preferred_element_type=j...  6.22 us
    ppermute x2, starting transfers between devices, padded_2(): after = lax.ppermute(initial, axis, down)  2.58 us
    dot_general x2, matrix products, project_angle(): jnp.einsum('zrtc,rcd->ztd', moved, tiles[:, k], preferred_element_type=jn...  2.35 us
    ppermute x2, waiting for transfers between devices, padded_2(): after = lax.ppermute(initial, axis, down)  2.24 us
    gather x6, local copies, waits for them, and re-layouts, spread_angle(): lax.dynamic_slice_in_dim(view_pad, margin - offset, tile_count, 1)  2.22 us
  transfers between devices with their start and end apart: 5, of which 2 were waited for; matrix products, arithmetic and copies ran while one was open for 2% of the time, Pallas kernels for 0%

commit v1 on v0

v1 whole, which is shorter than its diff:
```python
import functools

import jax
import jax.numpy as jnp
from jax import lax
from jax.experimental import pallas as pl
from jax.experimental.pallas import tpu as pltpu
from jax.sharding import PartitionSpec as P

OFFMAX = 3

step_size = 0.3
smooth_weight = 0.2
smooth_floor = 0.25

F32 = jnp.float32
BF16 = jnp.bfloat16


def kernel(
    slabs,
    n,
    vol_hbm,
    meas_hbm,
    tiles_hbm,
    off_ref,
    cnt_ref,
    upd_ref,
    res_ref,
    vol_in,
    meas,
    tiles,
    vol32,
    volt,
    part_own,
    sib_send,
    sib_recv,
    chip_send,
    chip_recv,
    same_recv,
    sibres_recv,
    own_res,
    respad,
    grad,
    base,
    flow_low,
    ys,
    yr,
    zr,
    cr,
    load_sem,
    sib_ssem,
    sib_rsem,
    chip_ssem,
    chip_rsem,
    same_ssem,
    same_rsem,
    sr_ssem,
    sr_rsem,
    y_ssem,
    y_rsem,
    z_ssem,
    z_rsem,
    c_ssem,
    c_rsem,
):
    depth, rows, width = vol_in.shape
    band = tiles.shape[2]
    tile = tiles.shape[3]
    tcount = width // tile
    flat = tcount * depth
    center = band // 2
    margin = OFFMAX + band
    zero_start = margin + tcount
    chips = n // 2

    slab = lax.axis_index("slab")
    me = lax.axis_index("angle")
    chip = lax.div(me, 2)
    core = lax.rem(me, 2)
    sib = me + 1 - 2 * core
    far_y = me - 1 + 2 * core
    first_row = me * rows
    barrier = pltpu.get_barrier_semaphore()

    has_far = (far_y >= 0) & (far_y < n)
    has_zp = slab + 1 < slabs
    has_zm = slab >= 1
    has_yp = me + 1 < n
    has_ym = me >= 1
    has_up = has_zp & has_ym
    has_down = has_zm & has_yp

    def greet(s, a):
        pl.semaphore_signal(barrier, inc=1, device_id=(s, a), device_id_type=pl.DeviceIdType.MESH)

    greet(slab, sib)
    for j in range(1, chips):
        greet(slab, 2 * lax.rem(chip + j, chips) + core)

    pl.when(has_far)(lambda: greet(slab, far_y))
    pl.when(has_zp)(lambda: greet(slab + 1, me))
    pl.when(has_zm)(lambda: greet(slab - 1, me))
    pl.when(has_up)(lambda: greet(slab + 1, me - 1))
    pl.when(has_down)(lambda: greet(slab - 1, me + 1))

    vol_copy = pltpu.make_async_copy(vol_hbm, vol_in, load_sem.at[0])
    vol_copy.start()
    order = [chips // 2] + [j for j in range(1, chips) if j != chips // 2] + [0]
    dest = [lax.rem(chip + j, chips) for j in order]
    loads = []
    for i in range(chips):
        pair = []
        for angle, slot in ((2 * dest[i] + 1 - core, 0), (2 * dest[i] + core, 1)):
            copy = pltpu.make_async_copy(
                tiles_hbm.at[angle], tiles.at[angle], load_sem.at[2 + 2 * i + slot]
            )
            copy.start()
            pair.append(copy)
        loads.append(pair)
    meas_copy = pltpu.make_async_copy(meas_hbm, meas, load_sem.at[1])
    meas_copy.start()

    volt[:, :margin] = jnp.zeros((rows, margin, depth, tile), F32)
    volt[:, zero_start:] = jnp.zeros((rows, volt.shape[1] - zero_start, depth, tile), F32)
    respad[:, :margin] = jnp.zeros((2, margin, depth, tile), F32)
    respad[:, zero_start:] = jnp.zeros((2, respad.shape[1] - zero_start, depth, tile), F32)
    vol_copy.wait()
    vol32[...] = vol_in[...].astype(F32)
    for y in range(rows):
        for t in range(tcount):
            volt[y, margin + t] = vol32[:, y, t * tile : (t + 1) * tile]

    def own_row(y):
        return volt[y, margin : margin + tcount].reshape(flat, tile)

    ys[0] = own_row(0).astype(BF16)
    ys[1] = own_row(rows - 1).astype(BF16)

    def send(src, dst, ssem, rsem, s, a):
        return pltpu.make_async_remote_copy(
            src_ref=src,
            dst_ref=dst,
            send_sem=ssem,
            recv_sem=rsem,
            device_id=(s, a),
            device_id_type=pl.DeviceIdType.MESH,
        )

    one = jnp.int32(1)
    none = jnp.int32(0)
    expect = jnp.int32(chips)
    for there in (has_far, has_zp, has_zm, has_up, has_down):
        expect = expect + jnp.where(there, one, none)
    pl.semaphore_wait(barrier, expect)

    halos = (
        (has_ym, send(ys.at[0], yr.at[1], y_ssem.at[0], y_rsem.at[1], slab, me - 1)),
        (has_yp, send(ys.at[1], yr.at[0], y_ssem.at[1], y_rsem.at[0], slab, me + 1)),
        (has_zm, send(vol32.at[0], zr.at[1], z_ssem.at[0], z_rsem.at[1], slab - 1, me)),
        (has_zp, send(vol32.at[depth - 1], zr.at[0], z_ssem.at[1], z_rsem.at[0], slab + 1, me)),
        (has_down, send(vol32.at[0], cr.at[1], c_ssem.at[0], c_rsem.at[1], slab - 1, me + 1)),
        (has_up, send(vol32.at[depth - 1], cr.at[0], c_ssem.at[1], c_rsem.at[0], slab + 1, me - 1)),
    )
    arrivals = (
        (has_yp, yr.at[1], send(ys.at[0], yr.at[1], y_ssem.at[0], y_rsem.at[1], slab, me + 1)),
        (has_ym, yr.at[0], send(ys.at[1], yr.at[0], y_ssem.at[1], y_rsem.at[0], slab, me - 1)),
        (has_zp, zr.at[1], send(vol32.at[0], zr.at[1], z_ssem.at[0], z_rsem.at[1], slab + 1, me)),
        (has_zm, zr.at[0], send(vol32.at[depth - 1], zr.at[0], z_ssem.at[1], z_rsem.at[0], slab - 1, me)),
        (has_up, cr.at[1], send(vol32.at[0], cr.at[1], c_ssem.at[0], c_rsem.at[1], slab + 1, me - 1)),
        (has_down, cr.at[0], send(vol32.at[depth - 1], cr.at[0], c_ssem.at[1], c_rsem.at[0], slab - 1, me + 1)),
    )
    for there, copy in halos:
        pl.when(there)(copy.start)

    def starts(angle, y, sign):
        found = []
        for k in range(band):
            shift = off_ref[angle, first_row + y] + (k - center)
            used = cnt_ref[angle, first_row + y] > k
            found.append(jnp.where(used, margin + sign * shift, zero_start))
        return found

    def view(angle):
        pieces = []
        for y in range(rows):
            for start in starts(angle, y, 1):
                pieces.append(volt[y, pl.ds(start, tcount)].reshape(flat, tile).astype(BF16))
        weights = tiles[angle].reshape(rows * band * tile, tile)
        return jnp.dot(jnp.concatenate(pieces, axis=1), weights, preferred_element_type=F32)

    def sib_copy(i):
        return send(sib_send.at[i], sib_recv.at[i], sib_ssem.at[i], sib_rsem.at[i], slab, sib)

    def chip_copy(i):
        return send(
            chip_send.at[i], chip_recv.at[i], chip_ssem.at[i], chip_rsem.at[i], slab, 2 * dest[i] + core
        )

    def for_sibling(i):
        loads[i][0].wait()
        sib_send[i] = view(2 * dest[i] + 1 - core)
        sib_copy(i).start()

    for_sibling(0)
    for i in range(chips):
        if i + 1 < chips:
            for_sibling(i + 1)
        loads[i][1].wait()
        part_own[...] = view(2 * dest[i] + core)
        sib_copy(i).wait_recv()
        if i + 1 < chips:
            chip_send[i] = part_own[...] + sib_recv[i]
            chip_copy(i).start()
        else:
            part_own[...] = part_own[...] + sib_recv[i]

    for there, buffer, copy in arrivals:
        pl.when(there)(copy.wait_recv)

        @pl.when(jnp.logical_not(there))
        def _(buffer=buffer):
            buffer[...] = jnp.zeros(buffer.shape, buffer.dtype)

    lane = lax.broadcasted_iota(jnp.int32, (flat + depth, tile), 1)
    level = lax.rem(lax.broadcasted_iota(jnp.int32, (flat + depth, tile), 0), depth)
    zeros_tile = jnp.zeros((depth, tile), F32)

    low = zr[0]
    low_y = jnp.concatenate([low[1:], cr[0][:1]], axis=0)
    low_lane = lax.broadcasted_iota(jnp.int32, (rows, width), 1)
    low_x = jnp.where(low_lane == width - 1, 0.0, pltpu.roll(low, width - 1, 1))
    lz, ly, lx = vol32[0] - low, low_y - low, low_x - low
    flow_low[...] = lz * lax.rsqrt(lz * lz + ly * ly + lx * lx + smooth_floor)

    def field_row(y):
        if 0 <= y < rows:
            return volt[y, margin - 1 : margin + tcount + 1].reshape(flat + 2 * depth, tile)
        inner = yr[0 if y < 0 else 1].astype(F32)
        return jnp.concatenate([zeros_tile, inner, zeros_tile], axis=0)

    def spread_row(ref, row):
        return [
            jnp.broadcast_to(ref[row : row + 1, t * tile : (t + 1) * tile], (depth, tile))
            for t in range(tcount)
        ]

    def flow(y):
        wide = field_row(y)
        here = wide[: flat + depth]
        rolled = pltpu.roll(wide, tile - 1, 1)
        dx = jnp.where(lane == tile - 1, rolled[depth:], rolled[: flat + depth]) - here
        dy = field_row(y + 1)[: flat + depth] - here
        top = spread_row(zr.at[1], y) if y >= 0 else spread_row(cr.at[1], rows - 1)
        top = jnp.concatenate([zeros_tile] + top, axis=0)
        dz = jnp.where(level == depth - 1, top, pltpu.roll(here, flat + depth - 1, 0)) - here
        inv = lax.rsqrt(dz * dz + dy * dy + dx * dx + smooth_floor)
        return dz * inv, dy * inv, dx * inv

    before = flow(-1)[1][depth:]
    for y in range(rows):
        fz, fy, fx = flow(y)
        fz, fy = fz[depth:], fy[depth:]
        under = jnp.concatenate(spread_row(flow_low, y), axis=0)
        div = fz - jnp.where(level[:flat] == 0, under, pltpu.roll(fz, 1, 0))
        div = div + (fy - before)
        rolled = pltpu.roll(fx, 1, 1)
        div = div + (fx[depth:] - jnp.where(lane[:flat] == 0, rolled[:flat], rolled[depth:]))
        base[y] = own_row(y) + step_size * smooth_weight * div
        before = fy

    total = part_own[...]
    for i in range(chips - 1):
        chip_copy(i).wait_recv()
        total = total + chip_recv[i]
    meas_copy.wait()
    total = total.reshape(tcount, depth, tile)
    for t in range(tcount):
        here = total[t] - meas[0, :, t * tile : (t + 1) * tile]
        res_ref[0, :, t * tile : (t + 1) * tile] = here
        respad[0, margin + t] = here.astype(BF16).astype(F32)
    own_res[...] = respad[0, margin:zero_start].reshape(flat, tile).astype(BF16)

    def same_copy(i):
        return send(own_res, same_recv.at[i], same_ssem.at[i], same_rsem.at[i], slab, 2 * dest[i] + core)

    def forward(i):
        src = own_res if i == chips - 1 else same_recv.at[i]
        return send(src, sibres_recv.at[i], sr_ssem.at[i], sr_rsem.at[i], slab, sib)

    for i in range(chips - 1):
        same_copy(i).start()
    forward(chips - 1).start()

    def back(angle, slot, fresh):
        for y in range(rows):
            acc = None
            for k, start in enumerate(starts(angle, y, -1)):
                piece = respad[slot, pl.ds(start, tcount)].reshape(flat, tile).astype(BF16)
                product = lax.dot_general(
                    piece, tiles[angle, y, k], (((1,), (1,)), ((), ())), preferred_element_type=F32
                )
                acc = product if acc is None else acc + product
            grad[y] = acc if fresh else grad[y] + acc

    def take(block, slot):
        respad[slot, margin:zero_start] = block.astype(F32).reshape(tcount, depth, tile)

    back(me, 0, True)
    forward(chips - 1).wait_recv()
    take(sibres_recv[chips - 1], 1)
    back(sib, 1, False)
    for i in range(chips - 1):
        source = lax.rem(chip + chips - order[i], chips)
        same_copy(i).wait_recv()
        forward(i).start()
        take(same_recv[i], 0)
        back(2 * source + core, 0, False)
        forward(i).wait_recv()
        take(sibres_recv[i], 1)
        back(2 * source + 1 - core, 1, False)

    for y in range(rows):
        out = (base[y] - step_size * grad[y]).reshape(tcount, depth, tile)
        for t in range(tcount):
            upd_ref[:, y, t * tile : (t + 1) * tile] = out[t]

    for there, copy in halos:
        pl.when(there)(copy.wait_send)
    for i in range(chips):
        sib_copy(i).wait_send()
        forward(i).wait_send()
    for i in range(chips - 1):
        chip_copy(i).wait_send()
        same_copy(i).wait_send()


def per_device(slabs, n, volume, measured, ray_tiles, tile_offsets, band_counts):
    depth, rows, width = volume.shape
    count, unused, band, tile, unused_2 = ray_tiles.shape
    tcount = width // tile
    flat = tcount * depth
    padded = 2 * tcount + OFFMAX + band
    chips = n // 2
    dma = pltpu.SemaphoreType.DMA
    vmem = pltpu.VMEM
    block = (flat, tile)
    return pl.pallas_call(
        functools.partial(kernel, slabs, n),
        out_shape=(
            jax.ShapeDtypeStruct(volume.shape, F32),
            jax.ShapeDtypeStruct(measured.shape, F32),
        ),
        in_specs=[pl.BlockSpec(memory_space=pl.ANY)] * 3
        + [pl.BlockSpec(memory_space=pltpu.SMEM)] * 2,
        out_specs=(pl.BlockSpec(memory_space=pltpu.VMEM),) * 2,
        scratch_shapes=[
            vmem(volume.shape, BF16),
            vmem(measured.shape, F32),
            vmem(ray_tiles.shape, BF16),
            vmem(volume.shape, F32),
            vmem((rows, padded, depth, tile), F32),
            vmem(block, F32),
            vmem((chips, *block), F32),
            vmem((chips, *block), F32),
            vmem((chips - 1, *block), F32),
            vmem((chips - 1, *block), F32),
            vmem((chips - 1, *block), BF16),
            vmem((chips, *block), BF16),
            vmem(block, BF16),
            vmem((2, padded, depth, tile), F32),
            vmem((rows, *block), F32),
            vmem((rows, *block), F32),
            vmem((rows, width), F32),
            vmem((2, *block), BF16),
            vmem((2, *block), BF16),
            vmem((2, rows, width), F32),
            vmem((2, rows, width), F32),
            dma((2 + n,)),
            dma((chips,)),
            dma((chips,)),
            dma((chips - 1,)),
            dma((chips - 1,)),
            dma((chips - 1,)),
            dma((chips - 1,)),
            dma((chips,)),
            dma((chips,)),
            dma((2,)),
            dma((2,)),
            dma((2,)),
            dma((2,)),
            dma((2,)),
            dma((2,)),
        ],
        compiler_params=pltpu.CompilerParams(
            collective_id=0, has_side_effects=True, vmem_limit_bytes=40 * 1024 * 1024
        ),
        name="step",
    )(volume, measured, ray_tiles, tile_offsets, band_counts)


def solution(mesh):
    return jax.shard_map(
        functools.partial(per_device, mesh.shape["slab"], mesh.shape["angle"]),
        mesh=mesh,
        in_specs=(
            P("slab", "angle", None),
            P("angle", "slab", None),
            P(None, "angle", None, None, None),
            P(),
            P(),
        ),
        out_specs=(P("slab", "angle", None), P("angle", "slab", None)),
        check_vma=False,
    )
```

time: 97.1 us -> 29.8 us (0.31)
  waiting for transfers between devices: 31.7 us -> 0 us
  Pallas kernels: 0 us -> 22.6 us
  blocking collectives: 15.9 us -> 0 us
  between operations: 14.3 us -> 0.65 us
  starting transfers between devices: 9.72 us -> 0 us
  matrix products: 8.57 us -> 0 us
  other arithmetic: 6.94 us -> 0 us
  local copies, waits for them, and re-layouts: 9.46 us -> 6.03 us
    psum x1 -> x0, waiting for transfers between devices: 29.5 us -> none  [per_device(): lax.psum(jax.vmap(partial(project_angle, margin=margin), in_axes=(None, 0...]
    pallas_call x0 -> x1, Pallas kernels: none -> 22.6 us  [per_device(): pl.pallas_call(functools.partial(kernel, slabs, n), out_shape=(jax.ShapeD...]
    all_gather x1 -> x0, blocking collectives: 15.9 us -> none  [per_device(): measured_all = lax.all_gather(measured, 'angle', axis=0, tiled=True)]
    ppermute x4 -> x0, starting transfers between devices: 9.68 us -> none  [the longest x2 7.09 us: padded_2(): before = lax.ppermute(last, axis, up)]
    dot_general x4 -> x0, matrix products: 8.57 us -> none  [the longest x2 6.22 us: spread_angle(): jnp.einsum('zrtd,rcd->zrtc', moved, tiles[:, k], preferred_element_type=j...]
    unnamed x10 -> x12, local copies, waits for them, and re-layouts: 0.12 us -> 6.03 us
    gather x12 -> x0, local copies, waits for them, and re-layouts: 4.37 us -> none  [the longest x6 2.22 us: spread_angle(): lax.dynamic_slice_in_dim(view_pad, margin - offset, tile_count, 1)]
    ppermute x4 -> x0, waiting for transfers between devices: 2.25 us -> none  [the longest x2 2.24 us: padded_2(): after = lax.ppermute(initial, axis, down)]
  transfers between devices with their start and end apart: 5 -> 0, of which waited for: 2 -> 0; matrix products, arithmetic and copies ran while one was open for 2% -> 0% of each run, Pallas kernels for 0% -> 0%
where the time goes in v1:
time: 29.8 us; the launch traced here: 29.3 us
  Pallas kernels  22.6 us (76%)
  local copies, waits for them, and re-layouts  6.03 us (20%)
  between operations  0.65 us (2%)
    pallas_call x1, Pallas kernels, per_device(): pl.pallas_call(functools.partial(kernel, slabs, n), out_shape=(jax.ShapeD...  22.6 us
    unnamed x12, local copies, waits for them, and re-layouts  6.03 us

profile of v1, /device:TPU:0, one launch (start us, length us, event | category | flops | bytes accessed | tf_op | source)
XLA Modules:
  0.0 29.3 jit_solution(6216644516058923785)
XLA Ops:
  0.6 0.0 copy-start
  0.6 1.6 %copy-done = bf16[8,4,2,128,128]{4,3,2,1,0:T(8,128)(2,1)S(1)} copy-done((bf16[8,4,2,128,128]{4,3,2,1,0:T(8,128)(2,1)S(1)}, bf16[8,4,2,128,128]{4,3,2,1,0:T(8,128)(2,1)}, u32[]{:S(2)}) %copy-start) | copy-done | bytes 2097176
  2.2 0.0 copy-start.1
  2.2 0.9 %copy-done.1 = bf16[8,4,2048]{2,1,0:T(4,128)(2,1)S(1)} copy-done((bf16[8,4,2048]{2,1,0:T(4,128)(2,1)S(1)}, bf16[8,4,2048]{2,1,0:T(4,128)(2,1)}, u32[]{:S(2)}) %copy-start.1) | copy-done | bytes 131096
  3.1 0.0 copy-start.2
  3.1 0.8 %copy-done.2 = f32[1,8,2048]{2,1,0:T(8,128)S(1)} copy-done((f32[1,8,2048]{2,1,0:T(8,128)S(1)}, f32[1,8,2048]{2,1,0:T(8,128)}, u32[]{:S(2)}) %copy-start.2) | copy-done | bytes 65560
  4.0 0.0 copy-start.3
  4.0 0.7 %copy-done.3 = s32[8,32]{1,0:T(8,128)S(1)} copy-done((s32[8,32]{1,0:T(8,128)S(1)}, s32[8,32]{1,0:T(8,128)}, u32[]{:S(2)}) %copy-start.3) | copy-done | bytes 1048
  4.7 0.0 copy-start.4
  4.7 0.7 %copy-done.4 = s32[8,32]{1,0:T(8,128)S(1)} copy-done((s32[8,32]{1,0:T(8,128)S(1)}, s32[8,32]{1,0:T(8,128)}, u32[]{:S(2)}) %copy-start.4) | copy-done | bytes 1048
  5.3 22.6 %step.1 = (f32[8,4,2048]{2,1,0:T(4,128)S(1)}, f32[1,8,2048]{2,1,0:T(8,128)S(1)}) custom-call(bf16[8,4,2048]{2,1,0:T(4,128)(2,1)S(1)} %copy-done.1, f32[1,8,2048]{2,1,0:T(8,128)S(1)} %copy-done.2, bf16[8,4,2,128,128]{4,3,2,1,0:T(8,128)(2,1)S(1)} %copy-done, s32[8,32]{1,0:T(8,128)S(1)} %copy-done.3, s32[8,32]{1,0:T(8,128)S(1)} %copy-done.4), custom_call_target="tpu_custom_call" | custom-call | tf_op jit(solution)/shard_map/step/pallas_call | solution.py:348
  27.9 0.7 %copy.9 = f32[8,4,2048]{2,1,0:T(4,128)} copy(f32[8,4,2048]{2,1,0:T(4,128)S(1)} %get-tuple-element.4) | data formatting | bytes 524288
  28.6 0.6 %copy.10 = f32[1,8,2048]{2,1,0:T(8,128)} copy(f32[1,8,2048]{2,1,0:T(8,128)S(1)} %get-tuple-element.5) | data formatting | bytes 131072
Async XLA Ops:
  0.6 1.6 %copy-start = (bf16[8,4,2,128,128]{4,3,2,1,0:T(8,128)(2,1)S(1)}, bf16[8,4,2,128,128]{4,3,2,1,0:T(8,128)(2,1)}, u32[]{:S(2)}) copy-start(bf16[8,4,2,128,128]{4,3,2,1,0:T(8,128)(2,1)} %tiles_hbm.1) | copy-start | bytes 6291460
  2.2 0.9 %copy-start.1 = (bf16[8,4,2048]{2,1,0:T(4,128)(2,1)S(1)}, bf16[8,4,2048]{2,1,0:T(4,128)(2,1)}, u32[]{:S(2)}) copy-start(bf16[8,4,2048]{2,1,0:T(4,128)(2,1)} %vol_hbm.1) | copy-start | bytes 393220
  3.1 0.8 %copy-start.2 = (f32[1,8,2048]{2,1,0:T(8,128)S(1)}, f32[1,8,2048]{2,1,0:T(8,128)}, u32[]{:S(2)}) copy-start(f32[1,8,2048]{2,1,0:T(8,128)} %meas_hbm.1) | copy-start | bytes 196612
  4.0 0.7 %copy-start.3 = (s32[8,32]{1,0:T(8,128)S(1)}, s32[8,32]{1,0:T(8,128)}, u32[]{:S(2)}) copy-start(s32[8,32]{1,0:T(8,128)} %off_ref.1) | copy-start | bytes 3076
  4.7 0.7 %copy-start.4 = (s32[8,32]{1,0:T(8,128)S(1)}, s32[8,32]{1,0:T(8,128)}, u32[]{:S(2)}) copy-start(s32[8,32]{1,0:T(8,128)} %cnt_ref.1) | copy-start | bytes 3076

commit v2 on v1

--- a/solution.py
+++ b/solution.py
@@ -23,8 +23,8 @@
     vol_hbm,
     meas_hbm,
     tiles_hbm,
-    off_ref,
-    cnt_ref,
+    off_hbm,
+    cnt_hbm,
     upd_ref,
     res_ref,
     vol_in,
@@ -48,6 +48,8 @@
     yr,
     zr,
     cr,
+    off_ref,
+    cnt_ref,
     load_sem,
     sib_ssem,
     sib_rsem,
@@ -106,6 +108,10 @@
 
     vol_copy = pltpu.make_async_copy(vol_hbm, vol_in, load_sem.at[0])
     vol_copy.start()
+    off_copy = pltpu.make_async_copy(off_hbm, off_ref, load_sem.at[n + 2])
+    off_copy.start()
+    cnt_copy = pltpu.make_async_copy(cnt_hbm, cnt_ref, load_sem.at[n + 3])
+    cnt_copy.start()
     order = [chips // 2] + [j for j in range(1, chips) if j != chips // 2] + [0]
     dest = [lax.rem(chip + j, chips) for j in order]
     loads = []
@@ -146,13 +152,6 @@
             device_id=(s, a),
             device_id_type=pl.DeviceIdType.MESH,
         )
-
-    one = jnp.int32(1)
-    none = jnp.int32(0)
-    expect = jnp.int32(chips)
-    for there in (has_far, has_zp, has_zm, has_up, has_down):
-        expect = expect + jnp.where(there, one, none)
-    pl.semaphore_wait(barrier, expect)
 
     halos = (
         (has_ym, send(ys.at[0], yr.at[1], y_ssem.at[0], y_rsem.at[1], slab, me - 1)),
@@ -170,9 +169,6 @@
         (has_up, cr.at[1], send(vol32.at[0], cr.at[1], c_ssem.at[0], c_rsem.at[1], slab + 1, me - 1)),
         (has_down, cr.at[0], send(vol32.at[depth - 1], cr.at[0], c_ssem.at[1], c_rsem.at[0], slab - 1, me + 1)),
     )
-    for there, copy in halos:
-        pl.when(there)(copy.start)
-
     def starts(angle, y, sign):
         found = []
         for k in range(band):
@@ -200,12 +196,26 @@
     def for_sibling(i):
         loads[i][0].wait()
         sib_send[i] = view(2 * dest[i] + 1 - core)
-        sib_copy(i).start()
-
+
+    off_copy.wait()
+    cnt_copy.wait()
     for_sibling(0)
+
+    one = jnp.int32(1)
+    none = jnp.int32(0)
+    expect = jnp.int32(chips)
+    for there in (has_far, has_zp, has_zm, has_up, has_down):
+        expect = expect + jnp.where(there, one, none)
+    pl.semaphore_wait(barrier, expect)
+
+    sib_copy(0).start()
+    for there, copy in halos:
+        pl.when(there)(copy.start)
+
     for i in range(chips):
         if i + 1 < chips:
             for_sibling(i + 1)
+            sib_copy(i + 1).start()
         loads[i][1].wait()
         part_own[...] = view(2 * dest[i] + core)
         sib_copy(i).wait_recv()
@@ -294,13 +304,17 @@
 
     def back(angle, slot, fresh):
         for y in range(rows):
-            acc = None
-            for k, start in enumerate(starts(angle, y, -1)):
-                piece = respad[slot, pl.ds(start, tcount)].reshape(flat, tile).astype(BF16)
-                product = lax.dot_general(
-                    piece, tiles[angle, y, k], (((1,), (1,)), ((), ())), preferred_element_type=F32
-                )
-                acc = product if acc is None else acc + product
+            pieces = [
+                respad[slot, pl.ds(start, tcount)].reshape(flat, tile).astype(BF16)
+                for start in starts(angle, y, -1)
+            ]
+            weights = jnp.concatenate([tiles[angle, y, k] for k in range(band)], axis=1)
+            acc = lax.dot_general(
+                jnp.concatenate(pieces, axis=1),
+                weights,
+                (((1,), (1,)), ((), ())),
+                preferred_element_type=F32,
+            )
             grad[y] = acc if fresh else grad[y] + acc
 
     def take(block, slot):
@@ -351,8 +365,7 @@
             jax.ShapeDtypeStruct(volume.shape, F32),
             jax.ShapeDtypeStruct(measured.shape, F32),
         ),
-        in_specs=[pl.BlockSpec(memory_space=pl.ANY)] * 3
-        + [pl.BlockSpec(memory_space=pltpu.SMEM)] * 2,
+        in_specs=[pl.BlockSpec(memory_space=pl.ANY)] * 5,
         out_specs=(pl.BlockSpec(memory_space=pltpu.VMEM),) * 2,
         scratch_shapes=[
             vmem(volume.shape, BF16),
@@ -376,7 +389,9 @@
             vmem((2, *block), BF16),
             vmem((2, rows, width), F32),
             vmem((2, rows, width), F32),
-            dma((2 + n,)),
+            pltpu.SMEM(tile_offsets.shape, jnp.int32),
+            pltpu.SMEM(band_counts.shape, jnp.int32),
+            dma((4 + n,)),
             dma((chips,)),
             dma((chips,)),
             dma((chips - 1,)),
@@ -393,7 +408,7 @@
             dma((2,)),
         ],
         compiler_params=pltpu.CompilerParams(
-            collective_id=0, has_side_effects=True, vmem_limit_bytes=40 * 1024 * 1024
+            collective_id=0, has_side_effects=True, vmem_limit_bytes=60 * 1024 * 1024
         ),
         name="step",
     )(volume, measured, ray_tiles, tile_offsets, band_counts)

time: 29.8 us -> 26.5 us (0.89)
  local copies, waits for them, and re-layouts: 6.03 us -> 3.14 us
  Pallas kernels: 22.6 us -> 22.3 us
    unnamed x12 -> x2, local copies, waits for them, and re-layouts: 6.03 us -> 3.14 us
where the time goes in v2:
time: 26.5 us; the launch traced here: 26.1 us
  Pallas kernels  22.3 us (84%)
  local copies, waits for them, and re-layouts  3.14 us (12%)
  between operations  0.64 us (2%)
    pallas_call x1, Pallas kernels, per_device(): pl.pallas_call(functools.partial(kernel, slabs, n), out_shape=(jax.ShapeD...  22.3 us
    unnamed x2, local copies, waits for them, and re-layouts  3.14 us

profile of v2, /device:TPU:0, one launch (start us, length us, event | category | flops | bytes accessed | tf_op | source)
XLA Modules:
  0.0 26.1 jit_solution(17957240724799145583)
XLA Ops:
  0.6 22.3 %step.1 = (f32[8,4,2048]{2,1,0:T(4,128)}, f32[1,8,2048]{2,1,0:T(8,128)}) custom-call(bf16[8,4,2048]{2,1,0:T(4,128)(2,1)} %vol_hbm.1, f32[1,8,2048]{2,1,0:T(8,128)} %meas_hbm.1, bf16[8,4,2,128,128]{4,3,2,1,0:T(8,128)(2,1)} %tiles_hbm.1, s32[8,32]{1,0:T(8,128)} %off_hbm.1, s32[8,32]{1,0:T(8,128)} %cnt_hbm.1), custom_call_target="tpu_custom_call" | custom-call | tf_op jit(solution)/shard_map/step/pallas_call | solution.py:362
  22.9 1.7 %copy.9 = f32[8,4,2048]{2,1,0:T(4,128)} copy(f32[8,4,2048]{2,1,0:T(4,128)} %get-tuple-element.4) | data formatting | bytes 524288
  24.6 1.5 %copy.10 = f32[1,8,2048]{2,1,0:T(8,128)} copy(f32[1,8,2048]{2,1,0:T(8,128)} %get-tuple-element.5) | data formatting | bytes 131072

commit v3 on v2

--- a/solution.py
+++ b/solution.py
@@ -25,6 +25,8 @@
     tiles_hbm,
     off_hbm,
     cnt_hbm,
+    upd_hbm,
+    res_hbm,
     upd_ref,
     res_ref,
     vol_in,
@@ -301,6 +303,8 @@
     for i in range(chips - 1):
         same_copy(i).start()
     forward(chips - 1).start()
+    res_copy = pltpu.make_async_copy(res_ref, res_hbm, load_sem.at[n + 4])
+    res_copy.start()
 
     def back(angle, slot, fresh):
         for y in range(rows):
@@ -338,6 +342,8 @@
         out = (base[y] - step_size * grad[y]).reshape(tcount, depth, tile)
         for t in range(tcount):
             upd_ref[:, y, t * tile : (t + 1) * tile] = out[t]
+    upd_copy = pltpu.make_async_copy(upd_ref, upd_hbm, load_sem.at[n + 5])
+    upd_copy.start()
 
     for there, copy in halos:
         pl.when(there)(copy.wait_send)
@@ -347,6 +353,19 @@
     for i in range(chips - 1):
         chip_copy(i).wait_send()
         same_copy(i).wait_send()
+    res_copy.wait()
+    upd_copy.wait()
+
+
+def finish(upd_ref, res_ref, upd_out, res_out, sem):
+    copies = (
+        pltpu.make_async_copy(upd_ref, upd_out, sem.at[0]),
+        pltpu.make_async_copy(res_ref, res_out, sem.at[1]),
+    )
+    for copy in copies:
+        copy.start()
+    for copy in copies:
+        copy.wait()
 
 
 def per_device(slabs, n, volume, measured, ray_tiles, tile_offsets, band_counts):
@@ -359,15 +378,18 @@
     dma = pltpu.SemaphoreType.DMA
     vmem = pltpu.VMEM
     block = (flat, tile)
-    return pl.pallas_call(
+    shapes = (
+        jax.ShapeDtypeStruct(volume.shape, F32),
+        jax.ShapeDtypeStruct(measured.shape, F32),
+    )
+    updated, residual = pl.pallas_call(
         functools.partial(kernel, slabs, n),
-        out_shape=(
-            jax.ShapeDtypeStruct(volume.shape, F32),
-            jax.ShapeDtypeStruct(measured.shape, F32),
-        ),
+        out_shape=shapes,
         in_specs=[pl.BlockSpec(memory_space=pl.ANY)] * 5,
-        out_specs=(pl.BlockSpec(memory_space=pltpu.VMEM),) * 2,
+        out_specs=(pl.BlockSpec(memory_space=pl.ANY),) * 2,
         scratch_shapes=[
+            vmem(volume.shape, F32),
+            vmem(measured.shape, F32),
             vmem(volume.shape, BF16),
             vmem(measured.shape, F32),
             vmem(ray_tiles.shape, BF16),
@@ -391,7 +413,7 @@
             vmem((2, rows, width), F32),
             pltpu.SMEM(tile_offsets.shape, jnp.int32),
             pltpu.SMEM(band_counts.shape, jnp.int32),
-            dma((4 + n,)),
+            dma((6 + n,)),
             dma((chips,)),
             dma((chips,)),
             dma((chips - 1,)),
@@ -412,6 +434,15 @@
         ),
         name="step",
     )(volume, measured, ray_tiles, tile_offsets, band_counts)
+    return pl.pallas_call(
+        finish,
+        out_shape=shapes,
+        in_specs=[pl.BlockSpec(memory_space=pl.ANY)] * 2,
+        out_specs=(pl.BlockSpec(memory_space=pl.ANY),) * 2,
+        scratch_shapes=[dma((2,))],
+        compiler_params=pltpu.CompilerParams(vmem_limit_bytes=60 * 1024 * 1024),
+        name="finish",
+    )(updated, residual)
 
 
 def solution(mesh):

time: 26.5 us -> 34.3 us (1.29)
  the two profiles are of different devices: /device:TPU:0 before, /device:TPU:1 now
where the time goes in v3:
time: 34.3 us; the launch traced here: 34.2 us
  Pallas kernels  33.5 us (98%)
  between operations  0.64 us (2%)
    pallas_call x1, Pallas kernels, per_device(): pl.pallas_call(functools.partial(kernel, slabs, n), out_shape=shapes, in_...  22.5 us
    pallas_call x1, Pallas kernels, per_device(): pl.pallas_call(finish, out_shape=shapes, in_specs=[pl.BlockSpec(memory_sp...  11 us

profile of v3, /device:TPU:1, one launch (start us, length us, event | category | flops | bytes accessed | tf_op | source)
XLA Modules:
  0.0 34.2 jit_solution(9889461130964571893)
XLA Ops:
  0.6 22.5 %step.1 = (f32[8,4,2048]{2,1,0:T(4,128)}, f32[1,8,2048]{2,1,0:T(8,128)}) custom-call(bf16[8,4,2048]{2,1,0:T(4,128)(2,1)} %vol_hbm.1, f32[1,8,2048]{2,1,0:T(8,128)} %meas_hbm.1, bf16[8,4,2,128,128]{4,3,2,1,0:T(8,128)(2,1)} %tiles_hbm.1, s32[8,32]{1,0:T(8,128)} %off_hbm.1, s32[8,32]{1,0:T(8,128)} %cnt_hbm.1), custom_call_target="tpu_custom_call" | custom-call | tf_op jit(solution)/shard_map/step/pallas_call | solution.py:385
  23.1 11.0 %finish.1 = (f32[8,4,2048]{2,1,0:T(4,128)}, f32[1,8,2048]{2,1,0:T(8,128)}) custom-call(f32[8,4,2048]{2,1,0:T(4,128)} %get-tuple-element.4.upd_ref, f32[1,8,2048]{2,1,0:T(8,128)} %get-tuple-element.5.res_ref), custom_call_target="tpu_custom_call" | custom-call | tf_op jit(solution)/shard_map/finish/pallas_call | solution.py:437

commit v4 on v3

--- a/solution.py
+++ b/solution.py
@@ -39,6 +39,7 @@
     sib_recv,
     chip_send,
     chip_recv,
+    relay_recv,
     same_recv,
     sibres_recv,
     own_res,
@@ -57,6 +58,7 @@
     sib_rsem,
     chip_ssem,
     chip_rsem,
+    relay_rsem,
     same_ssem,
     same_rsem,
     sr_ssem,
@@ -115,7 +117,15 @@
     cnt_copy = pltpu.make_async_copy(cnt_hbm, cnt_ref, load_sem.at[n + 3])
     cnt_copy.start()
     order = [chips // 2] + [j for j in range(1, chips) if j != chips // 2] + [0]
-    dest = [lax.rem(chip + j, chips) for j in order]
+    peer = [lax.rem(chip + j, chips) for j in order]
+    relayed = chips == 4
+    half = lax.div(chip, 2)
+    mate = chip + 1 - 2 * lax.rem(chip, 2)
+    middle = (chip >= 1) & (chip < chips - 1)
+    if relayed:
+        dest = [3 - 3 * half, 2 - half, mate, chip]
+    else:
+        dest = peer
     loads = []
     for i in range(chips):
         pair = []
@@ -201,6 +211,21 @@
 
     off_copy.wait()
     cnt_copy.wait()
+    def relay_copy(i):
+        return send(
+            chip_send.at[i], relay_recv.at[i], chip_ssem.at[i], relay_rsem.at[i], slab, 2 * mate + core
+        )
+
+    def far_copy(i):
+        return send(
+            chip_send.at[i], chip_recv.at[0], chip_ssem.at[i], chip_rsem.at[0], slab, 2 * dest[i] + core
+        )
+
+    def near_copy():
+        return send(
+            chip_send.at[2], chip_recv.at[1], chip_ssem.at[2], chip_rsem.at[1], slab, 2 * mate + core
+        )
+
     for_sibling(0)
 
     one = jnp.int32(1)
@@ -223,9 +248,23 @@
         sib_copy(i).wait_recv()
         if i + 1 < chips:
             chip_send[i] = part_own[...] + sib_recv[i]
-            chip_copy(i).start()
+            if not relayed:
+                chip_copy(i).start()
+            elif i < 2:
+                pl.when(jnp.logical_not(middle))(relay_copy(i).start)
+            else:
+                near_copy().start()
         else:
             part_own[...] = part_own[...] + sib_recv[i]
+
+    if relayed:
+
+        @pl.when(middle)
+        def _():
+            for i in range(2):
+                relay_copy(i).wait_recv()
+                chip_send[i] = chip_send[i] + relay_recv[i]
+                far_copy(i).start()
 
     for there, buffer, copy in arrivals:
         pl.when(there)(copy.wait_recv)
@@ -282,9 +321,15 @@
         before = fy
 
     total = part_own[...]
-    for i in range(chips - 1):
-        chip_copy(i).wait_recv()
-        total = total + chip_recv[i]
+    if relayed:
+        near_copy().wait_recv()
+        total = total + chip_recv[1]
+        far_copy(0).wait_recv()
+        total = total + chip_recv[0]
+    else:
+        for i in range(chips - 1):
+            chip_copy(i).wait_recv()
+            total = total + chip_recv[i]
     meas_copy.wait()
     total = total.reshape(tcount, depth, tile)
     for t in range(tcount):
@@ -294,7 +339,7 @@
     own_res[...] = respad[0, margin:zero_start].reshape(flat, tile).astype(BF16)
 
     def same_copy(i):
-        return send(own_res, same_recv.at[i], same_ssem.at[i], same_rsem.at[i], slab, 2 * dest[i] + core)
+        return send(own_res, same_recv.at[i], same_ssem.at[i], same_rsem.at[i], slab, 2 * peer[i] + core)
 
     def forward(i):
         src = own_res if i == chips - 1 else same_recv.at[i]
@@ -357,15 +402,22 @@
     upd_copy.wait()
 
 
-def finish(upd_ref, res_ref, upd_out, res_out, sem):
-    copies = (
-        pltpu.make_async_copy(upd_ref, upd_out, sem.at[0]),
-        pltpu.make_async_copy(res_ref, res_out, sem.at[1]),
-    )
-    for copy in copies:
-        copy.start()
-    for copy in copies:
-        copy.wait()
+def finish(upd_in, res_in, upd_out, res_out, upd, res, sem):
+    parts = sem.shape[1] - 1
+    size = upd.shape[0] // parts
+    pairs = [(res_in, res, res_out)]
+    for i in range(parts):
+        span = pl.ds(i * size, size)
+        pairs.append((upd_in.at[span], upd.at[span], upd_out.at[span]))
+    reads = [pltpu.make_async_copy(p[0], p[1], sem.at[0, i]) for i, p in enumerate(pairs)]
+    writes = [pltpu.make_async_copy(p[1], p[2], sem.at[1, i]) for i, p in enumerate(pairs)]
+    for read in reads:
+        read.start()
+    for read, write in zip(reads, writes):
+        read.wait()
+        write.start()
+    for write in writes:
+        write.wait()
 
 
 def per_device(slabs, n, volume, measured, ray_tiles, tile_offsets, band_counts):
@@ -400,6 +452,7 @@
             vmem((chips, *block), F32),
             vmem((chips - 1, *block), F32),
             vmem((chips - 1, *block), F32),
+            vmem((2, *block), F32),
             vmem((chips - 1, *block), BF16),
             vmem((chips, *block), BF16),
             vmem(block, BF16),
@@ -418,6 +471,7 @@
             dma((chips,)),
             dma((chips - 1,)),
             dma((chips - 1,)),
+            dma((2,)),
             dma((chips - 1,)),
             dma((chips - 1,)),
             dma((chips,)),
@@ -439,7 +493,7 @@
         out_shape=shapes,
         in_specs=[pl.BlockSpec(memory_space=pl.ANY)] * 2,
         out_specs=(pl.BlockSpec(memory_space=pl.ANY),) * 2,
-        scratch_shapes=[dma((2,))],
+        scratch_shapes=[vmem(volume.shape, F32), vmem(measured.shape, F32), dma((2, 5))],
         compiler_params=pltpu.CompilerParams(vmem_limit_bytes=60 * 1024 * 1024),
         name="finish",
     )(updated, residual)

time: 34.3 us -> 25.5 us (0.74)
  Pallas kernels: 33.5 us -> 24.6 us
    pallas_call x1, Pallas kernels: 11 us -> 1.68 us  [per_device(): pl.pallas_call(finish, out_shape=shapes, in_specs=[pl.BlockSpec(memory_sp...]
    pallas_call x1, Pallas kernels: 22.5 us -> 22.9 us  [per_device(): pl.pallas_call(functools.partial(kernel, slabs, n), out_shape=shapes, in_...]
where the time goes in v4:
time: 25.5 us; the launch traced here: 25.3 us
  Pallas kernels  24.6 us (96%)
  between operations  0.64 us (3%)
    pallas_call x1, Pallas kernels, per_device(): pl.pallas_call(functools.partial(kernel, slabs, n), out_shape=shapes, in_...  22.9 us
    pallas_call x1, Pallas kernels, per_device(): pl.pallas_call(finish, out_shape=shapes, in_specs=[pl.BlockSpec(memory_sp...  1.68 us

profile of v4, /device:TPU:1, one launch (start us, length us, event | category | flops | bytes accessed | tf_op | source)
XLA Modules:
  0.0 25.3 jit_solution(4274124631282921118)
XLA Ops:
  0.6 22.9 %step.1 = (f32[8,4,2048]{2,1,0:T(4,128)}, f32[1,8,2048]{2,1,0:T(8,128)}) custom-call(bf16[8,4,2048]{2,1,0:T(4,128)(2,1)} %vol_hbm.1, f32[1,8,2048]{2,1,0:T(8,128)} %meas_hbm.1, bf16[8,4,2,128,128]{4,3,2,1,0:T(8,128)(2,1)} %tiles_hbm.1, s32[8,32]{1,0:T(8,128)} %off_hbm.1, s32[8,32]{1,0:T(8,128)} %cnt_hbm.1), custom_call_target="tpu_custom_call" | custom-call | tf_op jit(solution)/shard_map/step/pallas_call | solution.py:437
  23.6 1.7 %finish.1 = (f32[8,4,2048]{2,1,0:T(4,128)}, f32[1,8,2048]{2,1,0:T(8,128)}) custom-call(f32[8,4,2048]{2,1,0:T(4,128)} %get-tuple-element.4.upd_in, f32[1,8,2048]{2,1,0:T(8,128)} %get-tuple-element.5.res_in), custom_call_target="tpu_custom_call" | custom-call | tf_op jit(solution)/shard_map/finish/pallas_call | solution.py:491

commit v5 on v3

--- a/solution.py
+++ b/solution.py
@@ -32,6 +32,7 @@
     vol_in,
     meas,
     tiles,
+    turned,
     vol32,
     volt,
     part_own,
@@ -227,6 +228,12 @@
         else:
             part_own[...] = part_own[...] + sib_recv[i]
 
+    @pl.loop(0, n)
+    def _(angle):
+        for y in range(rows):
+            for k in range(band):
+                turned[angle, y, k * tile : (k + 1) * tile] = tiles[angle, y, k].T
+
     for there, buffer, copy in arrivals:
         pl.when(there)(copy.wait_recv)
 
@@ -312,12 +319,8 @@
                 respad[slot, pl.ds(start, tcount)].reshape(flat, tile).astype(BF16)
                 for start in starts(angle, y, -1)
             ]
-            weights = jnp.concatenate([tiles[angle, y, k] for k in range(band)], axis=1)
-            acc = lax.dot_general(
-                jnp.concatenate(pieces, axis=1),
-                weights,
-                (((1,), (1,)), ((), ())),
-                preferred_element_type=F32,
+            acc = jnp.dot(
+                jnp.concatenate(pieces, axis=1), turned[angle, y], preferred_element_type=F32
             )
             grad[y] = acc if fresh else grad[y] + acc
 
@@ -357,15 +360,22 @@
     upd_copy.wait()
 
 
-def finish(upd_ref, res_ref, upd_out, res_out, sem):
-    copies = (
-        pltpu.make_async_copy(upd_ref, upd_out, sem.at[0]),
-        pltpu.make_async_copy(res_ref, res_out, sem.at[1]),
-    )
-    for copy in copies:
-        copy.start()
-    for copy in copies:
-        copy.wait()
+def finish(upd_in, res_in, upd_out, res_out, upd, res, sem):
+    parts = sem.shape[1] - 1
+    size = upd.shape[0] // parts
+    pairs = [(res_in, res, res_out)]
+    for i in range(parts):
+        span = pl.ds(i * size, size)
+        pairs.append((upd_in.at[span], upd.at[span], upd_out.at[span]))
+    reads = [pltpu.make_async_copy(p[0], p[1], sem.at[0, i]) for i, p in enumerate(pairs)]
+    writes = [pltpu.make_async_copy(p[1], p[2], sem.at[1, i]) for i, p in enumerate(pairs)]
+    for read in reads:
+        read.start()
+    for read, write in zip(reads, writes):
+        read.wait()
+        write.start()
+    for write in writes:
+        write.wait()
 
 
 def per_device(slabs, n, volume, measured, ray_tiles, tile_offsets, band_counts):
@@ -393,6 +403,7 @@
             vmem(volume.shape, BF16),
             vmem(measured.shape, F32),
             vmem(ray_tiles.shape, BF16),
+            vmem((n, rows, band * tile, tile), BF16),
             vmem(volume.shape, F32),
             vmem((rows, padded, depth, tile), F32),
             vmem(block, F32),
@@ -439,7 +450,7 @@
         out_shape=shapes,
         in_specs=[pl.BlockSpec(memory_space=pl.ANY)] * 2,
         out_specs=(pl.BlockSpec(memory_space=pl.ANY),) * 2,
-        scratch_shapes=[dma((2,))],
+        scratch_shapes=[vmem(volume.shape, F32), vmem(measured.shape, F32), dma((2, 5))],
         compiler_params=pltpu.CompilerParams(vmem_limit_bytes=60 * 1024 * 1024),
         name="finish",
     )(updated, residual)

time: 34.3 us -> 25.2 us (0.73)
  Pallas kernels: 33.5 us -> 24.4 us
    pallas_call x1, Pallas kernels: 11 us -> 1.68 us  [per_device(): pl.pallas_call(finish, out_shape=shapes, in_specs=[pl.BlockSpec(memory_sp...]
where the time goes in v5:
time: 25.2 us; the launch traced here: 25 us
  Pallas kernels  24.4 us (97%)
  between operations  0.64 us (3%)
    pallas_call x1, Pallas kernels, per_device(): pl.pallas_call(functools.partial(kernel, slabs, n), out_shape=shapes, in_...  22.7 us
    pallas_call x1, Pallas kernels, per_device(): pl.pallas_call(finish, out_shape=shapes, in_specs=[pl.BlockSpec(memory_sp...  1.68 us

profile of v5, /device:TPU:1, one launch (start us, length us, event | category | flops | bytes accessed | tf_op | source)
XLA Modules:
  0.0 25.0 jit_solution(4909584936950388340)
XLA Ops:
  0.6 22.7 %step.1 = (f32[8,4,2048]{2,1,0:T(4,128)}, f32[1,8,2048]{2,1,0:T(8,128)}) custom-call(bf16[8,4,2048]{2,1,0:T(4,128)(2,1)} %vol_hbm.1, f32[1,8,2048]{2,1,0:T(8,128)} %meas_hbm.1, bf16[8,4,2,128,128]{4,3,2,1,0:T(8,128)(2,1)} %tiles_hbm.1, s32[8,32]{1,0:T(8,128)} %off_hbm.1, s32[8,32]{1,0:T(8,128)} %cnt_hbm.1), custom_call_target="tpu_custom_call" | custom-call | tf_op jit(solution)/shard_map/step/pallas_call | solution.py:395
  23.3 1.7 %finish.1 = (f32[8,4,2048]{2,1,0:T(4,128)}, f32[1,8,2048]{2,1,0:T(8,128)}) custom-call(f32[8,4,2048]{2,1,0:T(4,128)} %get-tuple-element.4.upd_in, f32[1,8,2048]{2,1,0:T(8,128)} %get-tuple-element.5.res_in), custom_call_target="tpu_custom_call" | custom-call | tf_op jit(solution)/shard_map/finish/pallas_call | solution.py:448

commit v6 on v5

--- a/solution.py
+++ b/solution.py
@@ -8,6 +8,7 @@
 from jax.sharding import PartitionSpec as P
 
 OFFMAX = 3
+HALVES = 2
 
 step_size = 0.3
 smooth_weight = 0.2
@@ -32,7 +33,6 @@
     vol_in,
     meas,
     tiles,
-    turned,
     vol32,
     volt,
     part_own,
@@ -191,9 +191,19 @@
     def sib_copy(i):
         return send(sib_send.at[i], sib_recv.at[i], sib_ssem.at[i], sib_rsem.at[i], slab, sib)
 
-    def chip_copy(i):
+    part = flat // HALVES
+
+    def span(h):
+        return pl.ds(h * part, part)
+
+    def chip_copy(i, h):
         return send(
-            chip_send.at[i], chip_recv.at[i], chip_ssem.at[i], chip_rsem.at[i], slab, 2 * dest[i] + core
+            chip_send.at[i, span(h)],
+            chip_recv.at[i, span(h)],
+            chip_ssem.at[i, h],
+            chip_rsem.at[i, h],
+            slab,
+            2 * dest[i] + core,
         )
 
     def for_sibling(i):
@@ -224,15 +234,13 @@
         sib_copy(i).wait_recv()
         if i + 1 < chips:
             chip_send[i] = part_own[...] + sib_recv[i]
-            chip_copy(i).start()
+            chip_copy(i, 0).start()
         else:
             part_own[...] = part_own[...] + sib_recv[i]
 
-    @pl.loop(0, n)
-    def _(angle):
-        for y in range(rows):
-            for k in range(band):
-                turned[angle, y, k * tile : (k + 1) * tile] = tiles[angle, y, k].T
+    for h in range(1, HALVES):
+        for i in range(chips - 1):
+            chip_copy(i, h).start()
 
     for there, buffer, copy in arrivals:
         pl.when(there)(copy.wait_recv)
@@ -288,28 +296,38 @@
         base[y] = own_row(y) + step_size * smooth_weight * div
         before = fy
 
-    total = part_own[...]
-    for i in range(chips - 1):
-        chip_copy(i).wait_recv()
-        total = total + chip_recv[i]
+    def same_copy(i, h):
+        return send(
+            own_res.at[span(h)],
+            same_recv.at[i, span(h)],
+            same_ssem.at[i, h],
+            same_rsem.at[i, h],
+            slab,
+            2 * dest[i] + core,
+        )
+
+    def forward(i, h):
+        src = own_res.at[span(h)] if i == chips - 1 else same_recv.at[i, span(h)]
+        return send(src, sibres_recv.at[i, span(h)], sr_ssem.at[i, h], sr_rsem.at[i, h], slab, sib)
+
     meas_copy.wait()
-    total = total.reshape(tcount, depth, tile)
-    for t in range(tcount):
-        here = total[t] - meas[0, :, t * tile : (t + 1) * tile]
-        res_ref[0, :, t * tile : (t + 1) * tile] = here
-        respad[0, margin + t] = here.astype(BF16).astype(F32)
-    own_res[...] = respad[0, margin:zero_start].reshape(flat, tile).astype(BF16)
-
-    def same_copy(i):
-        return send(own_res, same_recv.at[i], same_ssem.at[i], same_rsem.at[i], slab, 2 * dest[i] + core)
-
-    def forward(i):
-        src = own_res if i == chips - 1 else same_recv.at[i]
-        return send(src, sibres_recv.at[i], sr_ssem.at[i], sr_rsem.at[i], slab, sib)
-
-    for i in range(chips - 1):
-        same_copy(i).start()
-    forward(chips - 1).start()
+    for h in range(HALVES):
+        total = part_own[span(h)]
+        for i in range(chips - 1):
+            chip_copy(i, h).wait_recv()
+            total = total + chip_recv[i, span(h)]
+        total = total.reshape(tcount // HALVES, depth, tile)
+        first = h * (tcount // HALVES)
+        for j in range(tcount // HALVES):
+            t = first + j
+            here = total[j] - meas[0, :, t * tile : (t + 1) * tile]
+            res_ref[0, :, t * tile : (t + 1) * tile] = here
+            respad[0, margin + t] = here.astype(BF16).astype(F32)
+        block = respad[0, margin + first : margin + first + tcount // HALVES]
+        own_res[span(h)] = block.reshape(part, tile).astype(BF16)
+        for i in range(chips - 1):
+            same_copy(i, h).start()
+        forward(chips - 1, h).start()
     res_copy = pltpu.make_async_copy(res_ref, res_hbm, load_sem.at[n + 4])
     res_copy.start()
 
@@ -319,27 +337,42 @@
                 respad[slot, pl.ds(start, tcount)].reshape(flat, tile).astype(BF16)
                 for start in starts(angle, y, -1)
             ]
-            acc = jnp.dot(
-                jnp.concatenate(pieces, axis=1), turned[angle, y], preferred_element_type=F32
+            weights = jnp.concatenate([tiles[angle, y, k] for k in range(band)], axis=1)
+            acc = lax.dot_general(
+                jnp.concatenate(pieces, axis=1),
+                weights,
+                (((1,), (1,)), ((), ())),
+                preferred_element_type=F32,
             )
             grad[y] = acc if fresh else grad[y] + acc
 
     def take(block, slot):
         respad[slot, margin:zero_start] = block.astype(F32).reshape(tcount, depth, tile)
 
+    source = [lax.rem(chip + chips - j, chips) for j in order]
+
+    def pass_on(i, h):
+        same_copy(i, h).wait_recv()
+        forward(i, h).start()
+
+    def from_sibling(i):
+        for h in range(HALVES):
+            forward(i, h).wait_recv()
+        take(sibres_recv[i], 1)
+        back(2 * source[i] + 1 - core, 1, False)
+
     back(me, 0, True)
-    forward(chips - 1).wait_recv()
-    take(sibres_recv[chips - 1], 1)
-    back(sib, 1, False)
+    for h in range(HALVES - 1):
+        for i in range(chips - 1):
+            pass_on(i, h)
+    from_sibling(chips - 1)
     for i in range(chips - 1):
-        source = lax.rem(chip + chips - order[i], chips)
-        same_copy(i).wait_recv()
-        forward(i).start()
+        pass_on(i, HALVES - 1)
         take(same_recv[i], 0)
-        back(2 * source + core, 0, False)
-        forward(i).wait_recv()
-        take(sibres_recv[i], 1)
-        back(2 * source + 1 - core, 1, False)
+        back(2 * source[i] + core, 0, False)
+        if i > 0:
+            from_sibling(i - 1)
+    from_sibling(chips - 2)
 
     for y in range(rows):
         out = (base[y] - step_size * grad[y]).reshape(tcount, depth, tile)
@@ -352,10 +385,11 @@
         pl.when(there)(copy.wait_send)
     for i in range(chips):
         sib_copy(i).wait_send()
-        forward(i).wait_send()
-    for i in range(chips - 1):
-        chip_copy(i).wait_send()
-        same_copy(i).wait_send()
+        for h in range(HALVES):
+            forward(i, h).wait_send()
+            if i + 1 < chips:
+                chip_copy(i, h).wait_send()
+                same_copy(i, h).wait_send()
     res_copy.wait()
     upd_copy.wait()
 
@@ -403,7 +437,6 @@
             vmem(volume.shape, BF16),
             vmem(measured.shape, F32),
             vmem(ray_tiles.shape, BF16),
-            vmem((n, rows, band * tile, tile), BF16),
             vmem(volume.shape, F32),
             vmem((rows, padded, depth, tile), F32),
             vmem(block, F32),
@@ -427,12 +460,12 @@
             dma((6 + n,)),
             dma((chips,)),
             dma((chips,)),
-            dma((chips - 1,)),
-            dma((chips - 1,)),
-            dma((chips - 1,)),
-            dma((chips - 1,)),
-            dma((chips,)),
-            dma((chips,)),
+            dma((chips - 1, HALVES)),
+            dma((chips - 1, HALVES)),
+            dma((chips - 1, HALVES)),
+            dma((chips - 1, HALVES)),
+            dma((chips, HALVES)),
+            dma((chips, HALVES)),
             dma((2,)),
             dma((2,)),
             dma((2,)),

time: 25.2 us -> 23.7 us (0.940)
  the two profiles are of different devices: /device:TPU:1 before, /device:TPU:0 now
where the time goes in v6:
time: 23.7 us; the launch traced here: 23.5 us
  Pallas kernels  22.8 us (96%)
  between operations  0.64 us (3%)
    pallas_call x1, Pallas kernels, per_device(): pl.pallas_call(functools.partial(kernel, slabs, n), out_shape=shapes, in_...  21.2 us
    pallas_call x1, Pallas kernels, per_device(): pl.pallas_call(finish, out_shape=shapes, in_specs=[pl.BlockSpec(memory_sp...  1.68 us

profile of v6, /device:TPU:0, one launch (start us, length us, event | category | flops | bytes accessed | tf_op | source)
XLA Modules:
  0.0 23.5 jit_solution(7791341514935311046)
XLA Ops:
  0.6 21.2 %step.1 = (f32[8,4,2048]{2,1,0:T(4,128)}, f32[1,8,2048]{2,1,0:T(8,128)}) custom-call(bf16[8,4,2048]{2,1,0:T(4,128)(2,1)} %vol_hbm.1, f32[1,8,2048]{2,1,0:T(8,128)} %meas_hbm.1, bf16[8,4,2,128,128]{4,3,2,1,0:T(8,128)(2,1)} %tiles_hbm.1, s32[8,32]{1,0:T(8,128)} %off_hbm.1, s32[8,32]{1,0:T(8,128)} %cnt_hbm.1), custom_call_target="tpu_custom_call" | custom-call | tf_op jit(solution)/shard_map/step/pallas_call | solution.py:429
  21.8 1.7 %finish.1 = (f32[8,4,2048]{2,1,0:T(4,128)}, f32[1,8,2048]{2,1,0:T(8,128)}) custom-call(f32[8,4,2048]{2,1,0:T(4,128)} %get-tuple-element.4.upd_in, f32[1,8,2048]{2,1,0:T(8,128)} %get-tuple-element.5.res_in), custom_call_target="tpu_custom_call" | custom-call | tf_op jit(solution)/shard_map/finish/pallas_call | solution.py:481

commit v7 on v6

--- a/solution.py
+++ b/solution.py
@@ -8,7 +8,7 @@
 from jax.sharding import PartitionSpec as P
 
 OFFMAX = 3
-HALVES = 2
+PARTS = 4
 
 step_size = 0.3
 smooth_weight = 0.2
@@ -191,7 +191,7 @@
     def sib_copy(i):
         return send(sib_send.at[i], sib_recv.at[i], sib_ssem.at[i], sib_rsem.at[i], slab, sib)
 
-    part = flat // HALVES
+    part = flat // PARTS
 
     def span(h):
         return pl.ds(h * part, part)
@@ -238,7 +238,7 @@
         else:
             part_own[...] = part_own[...] + sib_recv[i]
 
-    for h in range(1, HALVES):
+    for h in range(1, PARTS):
         for i in range(chips - 1):
             chip_copy(i, h).start()
 
@@ -311,19 +311,19 @@
         return send(src, sibres_recv.at[i, span(h)], sr_ssem.at[i, h], sr_rsem.at[i, h], slab, sib)
 
     meas_copy.wait()
-    for h in range(HALVES):
+    for h in range(PARTS):
         total = part_own[span(h)]
         for i in range(chips - 1):
             chip_copy(i, h).wait_recv()
             total = total + chip_recv[i, span(h)]
-        total = total.reshape(tcount // HALVES, depth, tile)
-        first = h * (tcount // HALVES)
-        for j in range(tcount // HALVES):
+        total = total.reshape(tcount // PARTS, depth, tile)
+        first = h * (tcount // PARTS)
+        for j in range(tcount // PARTS):
             t = first + j
             here = total[j] - meas[0, :, t * tile : (t + 1) * tile]
             res_ref[0, :, t * tile : (t + 1) * tile] = here
             respad[0, margin + t] = here.astype(BF16).astype(F32)
-        block = respad[0, margin + first : margin + first + tcount // HALVES]
+        block = respad[0, margin + first : margin + first + tcount // PARTS]
         own_res[span(h)] = block.reshape(part, tile).astype(BF16)
         for i in range(chips - 1):
             same_copy(i, h).start()
@@ -356,18 +356,18 @@
         forward(i, h).start()
 
     def from_sibling(i):
-        for h in range(HALVES):
+        for h in range(PARTS):
             forward(i, h).wait_recv()
         take(sibres_recv[i], 1)
         back(2 * source[i] + 1 - core, 1, False)
 
     back(me, 0, True)
-    for h in range(HALVES - 1):
+    for h in range(PARTS - 1):
         for i in range(chips - 1):
             pass_on(i, h)
     from_sibling(chips - 1)
     for i in range(chips - 1):
-        pass_on(i, HALVES - 1)
+        pass_on(i, PARTS - 1)
         take(same_recv[i], 0)
         back(2 * source[i] + core, 0, False)
         if i > 0:
@@ -385,7 +385,7 @@
         pl.when(there)(copy.wait_send)
     for i in range(chips):
         sib_copy(i).wait_send()
-        for h in range(HALVES):
+        for h in range(PARTS):
             forward(i, h).wait_send()
             if i + 1 < chips:
                 chip_copy(i, h).wait_send()
@@ -460,12 +460,12 @@
             dma((6 + n,)),
             dma((chips,)),
             dma((chips,)),
-            dma((chips - 1, HALVES)),
-            dma((chips - 1, HALVES)),
-            dma((chips - 1, HALVES)),
-            dma((chips - 1, HALVES)),
-            dma((chips, HALVES)),
-            dma((chips, HALVES)),
+            dma((chips - 1, PARTS)),
+            dma((chips - 1, PARTS)),
+            dma((chips - 1, PARTS)),
+            dma((chips - 1, PARTS)),
+            dma((chips, PARTS)),
+            dma((chips, PARTS)),
             dma((2,)),
             dma((2,)),
             dma((2,)),

time: 23.7 us -> 24.5 us (1.034)
  Pallas kernels: 22.8 us -> 23.7 us
    pallas_call x1, Pallas kernels: 21.2 us -> 22 us  [per_device(): pl.pallas_call(functools.partial(kernel, slabs, n), out_shape=shapes, in_...]
where the time goes in v7:
time: 24.5 us; the launch traced here: 24.3 us
  Pallas kernels  23.7 us (97%)
  between operations  0.64 us (3%)
    pallas_call x1, Pallas kernels, per_device(): pl.pallas_call(functools.partial(kernel, slabs, n), out_shape=shapes, in_...  22 us
    pallas_call x1, Pallas kernels, per_device(): pl.pallas_call(finish, out_shape=shapes, in_specs=[pl.BlockSpec(memory_sp...  1.68 us

profile of v7, /device:TPU:0, one launch (start us, length us, event | category | flops | bytes accessed | tf_op | source)
XLA Modules:
  0.0 24.3 jit_solution(3385679637441492705)
XLA Ops:
  0.6 22.0 %step.1 = (f32[8,4,2048]{2,1,0:T(4,128)}, f32[1,8,2048]{2,1,0:T(8,128)}) custom-call(bf16[8,4,2048]{2,1,0:T(4,128)(2,1)} %vol_hbm.1, f32[1,8,2048]{2,1,0:T(8,128)} %meas_hbm.1, bf16[8,4,2,128,128]{4,3,2,1,0:T(8,128)(2,1)} %tiles_hbm.1, s32[8,32]{1,0:T(8,128)} %off_hbm.1, s32[8,32]{1,0:T(8,128)} %cnt_hbm.1), custom_call_target="tpu_custom_call" | custom-call | tf_op jit(solution)/shard_map/step/pallas_call | solution.py:429
  22.6 1.7 %finish.1 = (f32[8,4,2048]{2,1,0:T(4,128)}, f32[1,8,2048]{2,1,0:T(8,128)}) custom-call(f32[8,4,2048]{2,1,0:T(4,128)} %get-tuple-element.4.upd_in, f32[1,8,2048]{2,1,0:T(8,128)} %get-tuple-element.5.res_in), custom_call_target="tpu_custom_call" | custom-call | tf_op jit(solution)/shard_map/finish/pallas_call | solution.py:481

commit v8 on v6

--- a/solution.py
+++ b/solution.py
@@ -117,6 +117,10 @@
     cnt_copy.start()
     order = [chips // 2] + [j for j in range(1, chips) if j != chips // 2] + [0]
     dest = [lax.rem(chip + j, chips) for j in order]
+    source = [lax.rem(chip + chips - j, chips) for j in order]
+    if chips == 4:
+        dest = [lax.rem(chip + 2, 4), 3 - chip, chip + 1 - 2 * lax.rem(chip, 2), chip]
+        source = dest
     loads = []
     for i in range(chips):
         pair = []
@@ -348,8 +352,6 @@
 
     def take(block, slot):
         respad[slot, margin:zero_start] = block.astype(F32).reshape(tcount, depth, tile)
-
-    source = [lax.rem(chip + chips - j, chips) for j in order]
 
     def pass_on(i, h):
         same_copy(i, h).wait_recv()

time: 23.7 us -> 23.3 us (0.983)
  Pallas kernels: 22.8 us -> 22.5 us
    pallas_call x1, Pallas kernels: 21.2 us -> 20.8 us  [per_device(): pl.pallas_call(functools.partial(kernel, slabs, n), out_shape=shapes, in_...]
where the time goes in v8:
time: 23.3 us; the launch traced here: 23.1 us
  Pallas kernels  22.5 us (97%)
  between operations  0.64 us (3%)
    pallas_call x1, Pallas kernels, per_device(): pl.pallas_call(functools.partial(kernel, slabs, n), out_shape=shapes, in_...  20.8 us
    pallas_call x1, Pallas kernels, per_device(): pl.pallas_call(finish, out_shape=shapes, in_specs=[pl.BlockSpec(memory_sp...  1.68 us

profile of v8, /device:TPU:0, one launch (start us, length us, event | category | flops | bytes accessed | tf_op | source)
XLA Modules:
  0.0 23.1 jit_solution(7091963631008218652)
XLA Ops:
  0.6 20.8 %step.1 = (f32[8,4,2048]{2,1,0:T(4,128)}, f32[1,8,2048]{2,1,0:T(8,128)}) custom-call(bf16[8,4,2048]{2,1,0:T(4,128)(2,1)} %vol_hbm.1, f32[1,8,2048]{2,1,0:T(8,128)} %meas_hbm.1, bf16[8,4,2,128,128]{4,3,2,1,0:T(8,128)(2,1)} %tiles_hbm.1, s32[8,32]{1,0:T(8,128)} %off_hbm.1, s32[8,32]{1,0:T(8,128)} %cnt_hbm.1), custom_call_target="tpu_custom_call" | custom-call | tf_op jit(solution)/shard_map/step/pallas_call | solution.py:431
  21.4 1.7 %finish.1 = (f32[8,4,2048]{2,1,0:T(4,128)}, f32[1,8,2048]{2,1,0:T(8,128)}) custom-call(f32[8,4,2048]{2,1,0:T(4,128)} %get-tuple-element.4.upd_in, f32[1,8,2048]{2,1,0:T(8,128)} %get-tuple-element.5.res_in), custom_call_target="tpu_custom_call" | custom-call | tf_op jit(solution)/shard_map/finish/pallas_call | solution.py:483
